TPU v7x, 32 devices: a whole 2x2x4 slice. The times are simulated.
32 devices in a mesh: groups: 2 (over y), expert: 4 (over z), dp: 4 (over x, core).
Axes of the slice: x: 2, y: 2, z: 4, core: 2. Of those that a mesh axis runs over, the one named last changes fastest.
Arguments:
- tokens: bfloat16 [512, 6144], P(('groups', 'expert'), 'dp'), parts along dimension 0, may hold values from -6 to 6
- expert_ids: int32 [512, 8], P(('groups', 'expert')), parts along dimension 0, may hold values from 0 to 31, all different within a row; in each aligned block of 64 rows (0 to 63, 64 to 127, ...) at most 32 rows name the same one
- scores: float32 [512, 8], P(('groups', 'expert')), parts along dimension 0, may hold values from -8 to 8
- w_gate: bfloat16 [32, 6144, 1024], P('expert', 'dp'), may hold values from -0.078125 to 0.078125
- w_up: bfloat16 [32, 6144, 1024], P('expert', 'dp'), may hold values from -0.078125 to 0.078125
- w_down: bfloat16 [32, 1024, 6144], P('expert', None, 'dp'), may hold values from -0.1875 to 0.1875
Outputs:
- mixed: bfloat16 [512, 6144], P(('groups', 'expert'), 'dp'), parts along dimension 0
There are 2 independent parts, one for each index of `groups`. A program takes and returns all parts, laid end to end along the dimension named above; an argument that names none is the same for every part. Nothing has to cross between parts.
Inputs may be any that keep to these rules, and one draw needn't show every extreme that they name: `expert_ids`: each row names 8 different experts; among the rows of one index of expert (aligned blocks of 64 rows) no expert is named by more than 32 rows, a bound that some block reaches.
All inputs are finite; a program needn't handle non-finite values.
Results may differ from a plain program's by a relative error of at most 0.024.
Values may be sent and summed in bfloat16 or wider, within the bound.
No kernel may reach another device: no remote copies, remote signals or barrier semaphores. Data moves between devices by JAX's collectives and lax.ppermute only.
A program may use at most 128 MiB of HBM per device.

v0:
```python
import jax
import jax.numpy as jnp
from jax import lax
from jax.sharding import PartitionSpec as P


def on_device(tokens, expert_ids, scores, w_gate, w_up, w_down):
    n_owner = lax.axis_size("expert")
    tok_rows, local_width = tokens.shape
    top = expert_ids.shape[1]
    experts_here = w_gate.shape[0]
    experts_all = experts_here * n_owner
    capacity = 2 * tok_rows * top // experts_all
    flat_ids = expert_ids.reshape(-1)
    onehot = (flat_ids[:, None] == jnp.arange(experts_all, dtype=jnp.int32)[None, :]).astype(
        jnp.int32
    )
    earlier = jnp.cumsum(onehot, axis=0) - onehot
    rank = jnp.sum(earlier * onehot, axis=1)
    slots = flat_ids * capacity + rank
    place = jnp.any(
        jnp.arange(experts_all * capacity, dtype=jnp.int32)[:, None, None]
        == slots.reshape(tok_rows, top)[None],
        axis=2,
    )
    buffer = jnp.dot(place.astype(jnp.bfloat16), tokens, preferred_element_type=jnp.float32).astype(
        jnp.bfloat16
    )
    buffer = buffer.reshape(n_owner, experts_here, capacity, local_width)
    received = lax.all_to_all(buffer, "expert", split_axis=0, concat_axis=0, tiled=True)
    gate_part = jnp.einsum("sjcd,jdh->sjch", received, w_gate, preferred_element_type=jnp.float32)
    up_part = jnp.einsum("sjcd,jdh->sjch", received, w_up, preferred_element_type=jnp.float32)
    gate = lax.psum_scatter(
        gate_part.astype(jnp.bfloat16), "dp", scatter_dimension=3, tiled=True
    ).astype(jnp.float32)
    up = lax.psum_scatter(
        up_part.astype(jnp.bfloat16), "dp", scatter_dimension=3, tiled=True
    ).astype(jnp.float32)
    share = (jax.nn.silu(gate) * up).astype(jnp.bfloat16)
    hidden = lax.all_gather(share, "dp", axis=3, tiled=True)
    expert_out = jnp.einsum(
        "sjch,jhd->sjcd", hidden, w_down, preferred_element_type=jnp.float32
    ).astype(jnp.bfloat16)
    returned = lax.all_to_all(expert_out, "expert", split_axis=0, concat_axis=0, tiled=True)
    returned = returned.reshape(experts_all * capacity, local_width)
    picked = returned[slots].reshape(tok_rows, top, local_width).astype(jnp.float32)
    affinity = jax.nn.sigmoid(scores)
    weights = 2.5 * affinity / jnp.sum(affinity, axis=1, keepdims=True)
    return jnp.einsum("tk,tkd->td", weights, picked).astype(jnp.bfloat16)


def solution(mesh):
    in_specs = (
        P(("groups", "expert"), "dp"),
        P(("groups", "expert"), None),
        P(("groups", "expert"), None),
        P("expert", "dp", None),
        P("expert", "dp", None),
        P("expert", None, "dp"),
    )
    out_specs = P(("groups", "expert"), "dp")
    return jax.shard_map(
        on_device, mesh=mesh, in_specs=in_specs, out_specs=out_specs, check_vma=False
    )
```

profile of v0, /device:TPU:0, one launch (start us, length us, event | category | flops | bytes accessed | tf_op | source)
XLA Modules:
  0.0 293.2 jit_solution(15262649235627956736)
XLA Ops:
  6.5 0.0 copy-start
  6.5 0.8 copy.22
  7.3 0.1 eq.43
  7.4 0.1 eq.39
  7.5 1.2 reduce-window.6
  8.7 0.2 slice_reduce_fusion
  9.0 0.1 fusion.32
  9.1 0.1 reduce_sum.24
  9.2 0.7 fusion.14
  9.9 1.0 convolution_convert_fusion
  11.0 76.8 %all_to_all.10 = bf16[4,8,32,1536]{3,2,1,0:T(8,128)(2,1)S(1)} all-to-all(bf16[4,8,32,1536]{3,2,1,0:T(8,128)(2,1)S(1)} %bitcast.65), channel_id=1, replica_groups=mesh['groups'=2,'expert'=4,'dp'=4] {'expert'}, dimensions={0} | all-to-all | bytes 6291456 | tf_op jit(solution)/shard_map/all_to_all | solution.py:30
  87.7 12.9 %convert_bitcast_fusion.1 = bf16[4,8,32,1024]{3,2,0,1:T(8,128)(2,1)} fusion(bf16[8,1536,1024]{2,1,0:T(8,128)(2,1)} %param.9, bf16[4,8,32,1536]{3,2,1,0:T(8,128)(2,1)S(1)} %all_to_all.10), kind=kOutput, calls=%fused_computation.13 | convolution fusion | flops 3222274048 | bytes 30408704 | tf_op jit(solution)/shard_map/sjcd,jdh->sjch/dot_general | solution.py:31
  100.7 0.0 reduce-scatter.3.cloned.1.call-update
  100.7 0.0 reduce-scatter.5.cloned.1.call-start
  100.8 13.8 %convert_bitcast_fusion = bf16[4,8,32,1024]{3,2,0,1:T(8,128)(2,1)} fusion(bf16[8,1536,1024]{2,1,0:T(8,128)(2,1)} %param.10, bf16[4,8,32,1536]{3,2,1,0:T(8,128)(2,1)S(1)} %all_to_all.10), kind=kOutput, calls=%fused_computation.12 | convolution fusion | flops 3222274048 | bytes 30408704 | tf_op jit(solution)/shard_map/sjcd,jdh->sjch/dot_general | solution.py:32
  114.6 0.0 reduce-scatter.5.cloned.1.call-update
  114.6 0.2 all-gather.2.cloned.1.call-start
  114.9 16.8 %reduce-scatter.3.cloned.1.call-done = bf16[4,8,32,256]{3,2,0,1:T(8,128)(2,1)} async-done(((bf16[4,8,32,1024]{3,2,0,1:T(8,128)(2,1)}), bf16[4,8,32,256]{3,2,0,1:T(8,128)(2,1)}) %reduce-scatter.3.cloned.1.call-update) | async-done | bytes 524304 | tf_op jit(solution)/shard_map/reduce_scatter | solution.py:33
  131.6 34.1 %reduce-scatter.5.cloned.1.call-done = bf16[4,8,32,256]{3,2,0,1:T(8,128)(2,1)} async-done(((bf16[4,8,32,1024]{3,2,0,1:T(8,128)(2,1)}), bf16[4,8,32,256]{3,2,0,1:T(8,128)(2,1)}) %reduce-scatter.5.cloned.1.call-update) | async-done | bytes 524304 | tf_op jit(solution)/shard_map/reduce_scatter | solution.py:36
  165.7 2.3 fusion.29
  168.1 0.0 all-gather.2.cloned.1.call-update
  168.1 23.0 %all-gather.2.cloned.1.call-done = bf16[4,8,32,1024]{3,2,0,1:T(8,128)(2,1)} async-done(((bf16[4,8,32,256]{3,2,0,1:T(8,128)(2,1)}), bf16[4,8,32,1024]{3,2,0,1:T(8,128)(2,1)}) %all-gather.2.cloned.1.call-update) | async-done | bytes 2097168 | tf_op jit(solution)/shard_map/all_gather | solution.py:40
  191.1 12.3 %fusion.9 = bf16[4,8,32,1536]{3,2,0,1:T(8,128)(2,1)S(1)} fusion(bf16[4,8,32,1024]{3,2,0,1:T(8,128)(2,1)} %all-gather.2.cloned.1.call-done, bf16[8,1024,1536]{2,1,0:T(8,128)(2,1)} %param.11), kind=kOutput, calls=%fused_computation.9 | convolution fusion | flops 3222798336 | bytes 30408704 | tf_op jit(solution)/shard_map/sjch,jhd->sjcd/dot_general | solution.py:41
  203.4 1.9 copy.28
  205.3 4.7 %all-to-all-start.1 = ((bf16[4,8,32,1536]{3,2,1,0:T(8,128)(2,1)}), bf16[4,8,32,1536]{3,2,1,0:T(8,128)(2,1)S(1)}, u32[]{:S(2)}, u32[]{:S(2)}) async-start(bf16[4,8,32,1536]{3,2,1,0:T(8,128)(2,1)} %copy.28), calls=%async_computation.3 | async-start | bytes 6291456 | tf_op jit(solution)/shard_map/all_to_all | solution.py:44
  210.0 0.1 mul.41
  210.1 0.0 copy-done.2
  210.1 0.1 copy.32
  210.3 70.8 %all-to-all-done.1 = bf16[4,8,32,1536]{3,2,1,0:T(8,128)(2,1)S(1)} async-done(((bf16[4,8,32,1536]{3,2,1,0:T(8,128)(2,1)}), bf16[4,8,32,1536]{3,2,1,0:T(8,128)(2,1)S(1)}, u32[]{:S(2)}, u32[]{:S(2)}) %all-to-all-start.1) | async-done | bytes 3145760 | tf_op jit(solution)/shard_map/all_to_all | solution.py:44
  281.1 3.0 %gather_fusion = bf16[512,1536]{1,0:T(8,128)(2,1)} fusion(bf16[1024,1536]{1,0:T(8,128)(2,1)S(1)} %bitcast.64, s32[1024]{0:T(1024)S(1)} %pad_clamp_fusion), kind=kCustom, calls=%fused_computation | custom fusion | bytes 3147776 | tf_op jit(solution)/shard_map/gather | solution.py:46
  284.0 2.0 fusion.23
  286.0 0.7 copy.45
  (13 shorter events, 0.1 us)
Async XLA Ops:
  6.5 3.4 %copy-start = (bf16[64,1536]{1,0:T(8,128)(2,1)S(1)}, bf16[64,1536]{1,0:T(8,128)(2,1)}, u32[]{:S(2)}) copy-start(bf16[64,1536]{1,0:T(8,128)(2,1)} %param.6) | copy-start | bytes 589828
  6.5 125.1 %reduce-scatter.3.cloned.1.call-start = ((), (), s32[]{:S(2)}) async-start(), calls=%async_computation.4 | async-start | bytes 2621440 | tf_op jit(solution)/shard_map/reduce_scatter | solution.py:33
  100.7 65.0 %reduce-scatter.5.cloned.1.call-start = ((), (), s32[]{:S(2)}) async-start(), calls=%async_computation.5 | async-start | bytes 2621440 | tf_op jit(solution)/shard_map/reduce_scatter | solution.py:36
  114.6 76.5 %all-gather.2.cloned.1.call-start = ((), (), s32[]{:S(2)}) async-start(), calls=%async_computation.6 | async-start | bytes 2621440 | tf_op jit(solution)/shard_map/all_gather | solution.py:40
  205.3 4.8 %copy-start.2 = (f32[64,8]{0,1:T(8,128)S(1)}, f32[64,8]{0,1:T(8,128)}, u32[]{:S(2)}) copy-start(f32[64,8]{0,1:T(8,128)} %param.8) | copy-start | bytes 6148
  205.3 75.8 %all-to-all-start.1 = ((bf16[4,8,32,1536]{3,2,1,0:T(8,128)(2,1)}), bf16[4,8,32,1536]{3,2,1,0:T(8,128)(2,1)S(1)}, u32[]{:S(2)}, u32[]{:S(2)}) async-start(bf16[4,8,32,1536]{3,2,1,0:T(8,128)(2,1)} %copy.28), calls=%async_computation.3 | async-start | bytes 6291456 | tf_op jit(solution)/shard_map/all_to_all | solution.py:44
  281.1 5.6 %copy-start.1 = (bf16[64,1536]{1,0:T(8,128)(2,1)S(1)}, bf16[64,1536]{1,0:T(8,128)(2,1)}, u32[]{:S(2)}) copy-start(bf16[64,1536]{1,0:T(8,128)(2,1)} %param.6) | copy-start | bytes 589828
Sparse Core Ops, SparseCore 0:
  100.8 30.7 reduce-scatter.2
  134.3 31.3 reduce-scatter.4
  168.2 22.8 all-gather.1
where the time goes:
time: 294 us; the launch traced here: 293 us
  waiting for transfers between devices  145 us (49%)
  blocking collectives  76.8 us (26%)
  matrix products  42 us (14%)
  between operations  13.2 us (4%)
  local copies, waits for them, and re-layouts  7.05 us (2%)
  starting transfers between devices  5 us (2%)
  other arithmetic  4.42 us (2%)
    all_to_all x1, blocking collectives, on_device(): lax.all_to_all(buffer, 'expert', split_axis=0, concat_axis=0, tiled=True)  76.8 us
    all_to_all x1, waiting for transfers between devices, on_device(): lax.all_to_all(expert_out, 'expert', split_axis=0, concat_axis=0, tiled=T...  70.8 us
    reduce_scatter x1, waiting for transfers between devices, on_device(): lax.psum_scatter(up_part.astype(jnp.bfloat16), 'dp', scatter_dimension=3,...  34.1 us
    all_gather x1, waiting for transfers between devices, on_device(): hidden = lax.all_gather(share, 'dp', axis=3, tiled=True)  23 us
    reduce_scatter x1, waiting for transfers between devices, on_device(): lax.psum_scatter(gate_part.astype(jnp.bfloat16), 'dp', scatter_dimension=...  16.8 us
    dot_general x1, matrix products, on_device(): jnp.einsum('sjcd,jdh->sjch', received, w_up, preferred_element_type=jnp.f...  13.8 us
    dot_general x1, matrix products, on_device(): jnp.einsum('sjcd,jdh->sjch', received, w_gate, preferred_element_type=jnp...  12.9 us
    dot_general x1, matrix products, on_device(): jnp.einsum('sjch,jhd->sjcd', hidden, w_down, preferred_element_type=jnp.f...  12.3 us
  transfers between devices with their start and end apart: 4, of which 4 were waited for; matrix products, arithmetic and copies ran while one was open for 5% of the time, Pallas kernels for 0%

commit v1 on v0

v1 whole, which is shorter than its diff:
```python
import functools

import jax
import jax.numpy as jnp
from jax import lax
from jax.experimental import pallas as pl
from jax.experimental.pallas import tpu as pltpu
from jax.sharding import PartitionSpec as P

LANES = 128
VMEM = pl.BlockSpec(memory_space=pltpu.VMEM)
SMEM = pl.BlockSpec(memory_space=pltpu.SMEM)
NOWHERE = -1e6


def bits_of(n):
    return [b for b in range(n.bit_length() - 1)]


def flip(x, axis, k):
    return lax.ppermute(x, axis, [(i, i ^ k) for i in range(lax.axis_size(axis))])


def route_body(n, experts, per_chunk, rows, info, *refs):
    meta, (rank_t, rank, wt, sched) = refs[:n], refs[n:]
    tok, top = meta[0].shape[0], meta[0].shape[1] // 2
    first = info[0].astype(jnp.float32)
    lane = lax.broadcasted_iota(jnp.int32, (tok, LANES), 1).astype(jnp.float32)
    before = (
        lax.broadcasted_iota(jnp.int32, (tok, tok), 0) > lax.broadcasted_iota(jnp.int32, (tok, tok), 1)
    ).astype(jnp.bfloat16)
    seen = jnp.zeros((1, LANES), jnp.float32)
    for s in range(n):
        block = meta[s][...]
        named = jnp.zeros((tok, LANES), jnp.float32)
        weight = jnp.zeros((tok, LANES), jnp.float32)
        for k in range(top):
            hit = jnp.where(block[:, k : k + 1] - first == lane, 1.0, 0.0)
            named = named + hit
            weight = weight + hit * block[:, top + k : top + k + 1]
        named = jnp.where(lane < experts, named, 0.0)
        place = jnp.dot(before, named.astype(jnp.bfloat16), preferred_element_type=jnp.float32) + seen
        rank[s * tok : (s + 1) * tok, :] = jnp.where(named > 0, place, NOWHERE)
        wt[s * tok : (s + 1) * tok, :] = weight
        seen = seen + jnp.sum(named, axis=0, keepdims=True)
    turned = jnp.transpose(rank[...])[: rank_t.shape[0]]
    rank_t[...] = turned
    count = jnp.sum((turned >= 0).astype(jnp.float32), axis=1, keepdims=True)
    shape = (rank_t.shape[0], LANES)
    j = lax.broadcasted_iota(jnp.int32, shape, 1).astype(jnp.float32)
    e = lax.broadcasted_iota(jnp.int32, shape, 0).astype(jnp.float32)
    ahead = ((seen > count) | ((seen == count) & (j < e))) & (j < experts)
    order = jnp.sum(ahead.astype(jnp.float32), axis=1, keepdims=True)
    large = jnp.where((order == j) & (e < experts), 1.0, 0.0)
    small = jnp.where((order == experts - 1 - j) & (e < experts), 1.0, 0.0)
    expert_a = jnp.sum(e * large, axis=0, keepdims=True)
    count_a = jnp.sum(count * large, axis=0, keepdims=True)
    if per_chunk == 2:
        expert_b = jnp.sum(e * small, axis=0, keepdims=True)
        count_b = jnp.sum(count * small, axis=0, keepdims=True)
    else:
        expert_b, count_b = expert_a, jnp.zeros_like(count_a)
        count_a = jnp.full_like(count_a, rows)
    sched[0:1] = expert_a.astype(jnp.int32)
    sched[1:2] = expert_b.astype(jnp.int32)
    sched[2:3] = count_a.astype(jnp.int32)
    sched[3:4] = (count_a + count_b).astype(jnp.int32)
    sched[4:8] = jnp.full((4, LANES), info[1], jnp.int32)


def route(meta, info, experts, per_chunk, rows):
    n, tok = len(meta), meta[0].shape[0]
    padded = -(-experts // 8) * 8
    return pl.pallas_call(
        functools.partial(route_body, n, experts, per_chunk, rows),
        out_shape=(
            jax.ShapeDtypeStruct((padded, n * tok), jnp.float32),
            jax.ShapeDtypeStruct((n * tok, LANES), jnp.float32),
            jax.ShapeDtypeStruct((n * tok, LANES), jnp.float32),
            jax.ShapeDtypeStruct((8, LANES), jnp.int32),
        ),
        in_specs=[SMEM] + [VMEM] * n,
        out_specs=(VMEM,) * 4,
        name="route",
    )(info, *meta)


def gate_up_body(n, chunk, half, sched, *refs):
    tokens, (rank_t, gate_a, gate_b, up_a, up_b, send, keep, feed, rows) = refs[:n], refs[n:]
    step = pl.program_id(0)
    count = rows.shape[0]
    split = sched[2, chunk]

    @pl.when(step == 0)
    def _():
        tok = tokens[0].shape[0]
        for s in range(n):
            feed[s * tok : (s + 1) * tok, :] = tokens[s][...]
        r = lax.broadcasted_iota(jnp.int32, (count, n * tok), 0).astype(jnp.float32)
        a = rank_t[pl.ds(sched[0, chunk], 1), :]
        b = rank_t[pl.ds(sched[1, chunk], 1), :] + split.astype(jnp.float32)
        pick = jnp.where(r == a, 1.0, 0.0) + jnp.where(r == b, 1.0, 0.0)
        rows[...] = jnp.dot(
            pick.astype(jnp.bfloat16), feed[...], preferred_element_type=jnp.float32
        ).astype(jnp.bfloat16)

    x = rows[...]
    width = gate_a.shape[2]
    of_a = lax.broadcasted_iota(jnp.int32, (count, width), 0) < split

    def both(wa, wb):
        left = jnp.dot(x, wa[0], preferred_element_type=jnp.float32)
        right = jnp.dot(x, wb[0], preferred_element_type=jnp.float32)
        return jnp.where(of_a, left, right).astype(jnp.bfloat16)

    gate, up = both(gate_a, gate_b), both(up_a, up_b)

    @pl.when(step < half)
    def _():
        send[0, :, :width] = gate
        send[0, :, width:] = up

    @pl.when(step >= half)
    def _():
        keep[0, :, :width] = gate
        keep[0, :, width:] = up


def gate_up(tokens, rank_t, sched, w_gate, w_up, chunk, rows, n_dp):
    n, (tok, local) = len(tokens), tokens[0].shape
    width = w_gate.shape[2] // n_dp
    half = max(n_dp // 2, 1)

    def weight_spec(row):
        def index(i, sched):
            part = jnp.where(i < half, 2 * i + 1, 2 * (i - half))
            return sched[row, chunk], 0, part ^ sched[4, 0]

        return pl.BlockSpec((1, local, width), index)

    whole = lambda shape: pl.BlockSpec(shape, lambda i, sched: (0, 0))
    out = jax.ShapeDtypeStruct((half, rows, 2 * width), jnp.bfloat16)
    flops = 2 * rows * local * 4 * width * n_dp
    return pl.pallas_call(
        functools.partial(gate_up_body, n, chunk, half),
        out_shape=(out, out),
        grid_spec=pltpu.PrefetchScalarGridSpec(
            num_scalar_prefetch=1,
            grid=(n_dp,),
            in_specs=[whole((tok, local))] * n
            + [whole(rank_t.shape)]
            + [weight_spec(0), weight_spec(1)] * 2,
            out_specs=(
                pl.BlockSpec((1, rows, 2 * width), lambda i, s: (jnp.minimum(i, half - 1), 0, 0)),
                pl.BlockSpec((1, rows, 2 * width), lambda i, s: (jnp.maximum(i - half, 0), 0, 0)),
            ),
            scratch_shapes=[
                pltpu.VMEM((n * tok, local), jnp.bfloat16),
                pltpu.VMEM((rows, local), jnp.bfloat16),
            ],
        ),
        compiler_params=pltpu.CompilerParams(vmem_limit_bytes=32 << 20),
        cost_estimate=pl.CostEstimate(
            flops=flops, bytes_accessed=2 * 4 * local * width * n_dp, transcendentals=0
        ),
        name="gate_up",
    )(sched, *tokens, rank_t, w_gate, w_gate, w_up, w_up)


def down_body(n_dp, n_out, chunk, first, sched, *refs):
    parts, (rank, wt, down_a, down_b), refs = refs[:n_dp], refs[n_dp : n_dp + 4], refs[n_dp + 4 :]
    before = None if first else refs[0]
    outs, (hidden, mix) = refs[0 if first else 1 : -2], refs[-2:]
    rows = hidden.shape[0]
    width = parts[0].shape[-1]
    split = sched[2, chunk]

    @pl.when(pl.program_id(0) == 0)
    def _():
        for l in range(n_dp):
            at = pl.multiple_of((l ^ sched[4, 0]) * width, width)
            hidden[:, pl.ds(at, width)] = parts[l][0]
        lane = lax.broadcasted_iota(jnp.int32, rank.shape, 1)
        column = lambda ref, e: jnp.sum(jnp.where(lane == e, ref[...], 0.0), axis=1, keepdims=True)
        r = lax.broadcasted_iota(jnp.int32, mix.shape, 1).astype(jnp.float32)
        a, b = sched[0, chunk], sched[1, chunk]
        place_b = column(rank, b) + split.astype(jnp.float32)
        mix[...] = (
            jnp.where(r == column(rank, a), column(wt, a), 0.0)
            + jnp.where(r == place_b, column(wt, b), 0.0)
        ).astype(jnp.bfloat16)

    left = jnp.dot(hidden[...], down_a[0], preferred_element_type=jnp.float32)
    right = jnp.dot(hidden[...], down_b[0], preferred_element_type=jnp.float32)
    of_a = lax.broadcasted_iota(jnp.int32, left.shape, 0) < split
    out = jnp.where(of_a, left, right).astype(jnp.bfloat16)
    total = jnp.dot(mix[...], out, preferred_element_type=jnp.float32)
    if not first:
        total = total + before[...]
    tok = total.shape[0] // n_out
    for s in range(n_out):
        outs[s][...] = total[s * tok : (s + 1) * tok].astype(outs[s].dtype)


def down(parts, rank, wt, sched, w_down, total, chunk, last, n_owner):
    n_dp = len(parts)
    _, rows, width = parts[0].shape
    _, hidden, local = w_down.shape
    tokens = rank.shape[0]
    block = 512 if local % 512 == 0 else 256 if local % 256 == 0 else local
    n_out = n_owner if last else 1
    kind = jnp.bfloat16 if last else jnp.float32
    first = total is None

    def weight_spec(row):
        return pl.BlockSpec((1, hidden, block), lambda i, s: (s[row, chunk], 0, i))

    whole = lambda shape: pl.BlockSpec(shape, lambda i, s: (0,) * len(shape))
    column = pl.BlockSpec((tokens, block), lambda i, s: (0, i))
    outs = pl.pallas_call(
        functools.partial(down_body, n_dp, n_out, chunk, first),
        out_shape=(jax.ShapeDtypeStruct((tokens // n_out, local), kind),) * n_out,
        grid_spec=pltpu.PrefetchScalarGridSpec(
            num_scalar_prefetch=1,
            grid=(local // block,),
            in_specs=[whole(parts[0].shape)] * n_dp
            + [whole(rank.shape)] * 2
            + [weight_spec(0), weight_spec(1)]
            + ([] if first else [column]),
            out_specs=(pl.BlockSpec((tokens // n_out, block), lambda i, s: (0, i)),) * n_out,
            scratch_shapes=[
                pltpu.VMEM((rows, hidden), jnp.bfloat16),
                pltpu.VMEM((tokens, rows), jnp.bfloat16),
            ],
        ),
        compiler_params=pltpu.CompilerParams(vmem_limit_bytes=48 << 20),
        cost_estimate=pl.CostEstimate(
            flops=2 * rows * local * (2 * hidden + tokens),
            bytes_accessed=2 * 2 * hidden * local + 8 * tokens * local,
            transcendentals=0,
        ),
        name="down",
    )(sched, *parts, rank, wt, w_down, w_down, *([] if first else [total]))
    return outs if last else outs[0]


def hidden_parts(send, keep, n_dp):
    bits = bits_of(n_dp)
    total = keep.astype(jnp.float32)
    for b in bits:
        if b > 0:
            send = total[1::2].astype(jnp.bfloat16)
            total = total[0::2]
        total = total + flip(send, "dp", 1 << b).astype(jnp.float32)
    width = total.shape[2] // 2
    share = (jax.nn.silu(total[:, :, :width]) * total[:, :, width:]).astype(jnp.bfloat16)
    parts = {0: share}
    for b in reversed(bits):
        for l in list(parts):
            parts[l | 1 << b] = flip(parts[l], "dp", 1 << b)
    return [parts[l] for l in range(n_dp)]


def on_device(tokens, expert_ids, scores, w_gate, w_up, w_down):
    n_owner, n_dp = lax.axis_size("expert"), lax.axis_size("dp")
    tok_rows, top = expert_ids.shape
    experts = w_gate.shape[0]
    capacity = 2 * tok_rows * top // (experts * n_owner)
    per_chunk = 2 if experts % 2 == 0 else 1
    rows = per_chunk * n_owner * capacity

    affinity = jax.nn.sigmoid(scores)
    weights = 2.5 * affinity / jnp.sum(affinity, axis=1, keepdims=True)
    meta = jnp.concatenate([expert_ids.astype(jnp.float32), weights], axis=1)
    metas = [meta] + [flip(meta, "expert", k) for k in range(1, n_owner)]
    feeds = [tokens] + [flip(tokens, "expert", k) for k in range(1, n_owner)]
    info = jnp.stack([lax.axis_index("expert") * experts, lax.axis_index("dp")]).astype(jnp.int32)
    rank_t, rank, wt, sched = route(metas, info, experts, per_chunk, rows)

    chunks = experts // per_chunk
    parts = [
        hidden_parts(*gate_up(feeds, rank_t, sched, w_gate, w_up, c, rows, n_dp), n_dp)
        for c in range(chunks)
    ]
    total = None
    for c in range(chunks):
        total = down(parts[c], rank, wt, sched, w_down, total, c, c == chunks - 1, n_owner)
    mixed = total[0].astype(jnp.float32)
    for k in range(1, n_owner):
        mixed = mixed + flip(total[k], "expert", k).astype(jnp.float32)
    return mixed.astype(jnp.bfloat16)


def solution(mesh):
    in_specs = (
        P(("groups", "expert"), "dp"),
        P(("groups", "expert"), None),
        P(("groups", "expert"), None),
        P("expert", "dp", None),
        P("expert", "dp", None),
        P("expert", None, "dp"),
    )
    out_specs = P(("groups", "expert"), "dp")
    return jax.shard_map(
        on_device, mesh=mesh, in_specs=in_specs, out_specs=out_specs, check_vma=False
    )
```

time: 294 us -> 143 us (0.49)
  waiting for transfers between devices: 145 us -> 44.4 us
  blocking collectives: 76.8 us -> 0 us
  Pallas kernels: 0 us -> 58.3 us
  matrix products: 42 us -> 0 us
  starting transfers between devices: 5 us -> 30.3 us
  between operations: 13.2 us -> 0.34 us
  local copies, waits for them, and re-layouts: 7.05 us -> 3.74 us
    all_to_all x1 -> x0, blocking collectives: 76.8 us -> none  [on_device(): lax.all_to_all(buffer, 'expert', split_axis=0, concat_axis=0, tiled=True)]
    all_to_all x1 -> x0, waiting for transfers between devices: 70.8 us -> none  [on_device(): lax.all_to_all(expert_out, 'expert', split_axis=0, concat_axis=0, tiled=T...]
    pallas_call x0 -> x9, Pallas kernels: none -> 58.3 us  [the longest x4 32.3 us: gate_up(): pl.pallas_call(functools.partial(gate_up_body, n, chunk, half), out_shape...]
    reduce_scatter x2 -> x0, waiting for transfers between devices: 50.9 us -> none  [the longest x1 34.1 us: on_device(): lax.psum_scatter(up_part.astype(jnp.bfloat16), 'dp', scatter_dimension=3,...]
    ppermute x0 -> x29, waiting for transfers between devices: none -> 44.4 us  [flip(): lax.ppermute(x, axis, [(i, i ^ k) for i in range(lax.axis_size(axis))])]
    dot_general x5 -> x0, matrix products: 42 us -> none  [the longest x1 13.8 us: on_device(): jnp.einsum('sjcd,jdh->sjch', received, w_up, preferred_element_type=jnp.f...]
    ppermute x0 -> x29, starting transfers between devices: none -> 30.3 us  [flip(): lax.ppermute(x, axis, [(i, i ^ k) for i in range(lax.axis_size(axis))])]
    all_gather x1 -> x0, waiting for transfers between devices: 23 us -> none  [on_device(): hidden = lax.all_gather(share, 'dp', axis=3, tiled=True)]
  transfers between devices with their start and end apart: 4 -> 29, of which waited for: 4 -> 10; matrix products, arithmetic and copies ran while one was open for 5% -> 3% of each run, Pallas kernels for 0% -> 31%
where the time goes in v1:
time: 143 us; the launch traced here: 142 us
  Pallas kernels  58.3 us (41%)
  waiting for transfers between devices  44.4 us (31%)
  starting transfers between devices  30.3 us (21%)
  other arithmetic  4.64 us (3%)
  local copies, waits for them, and re-layouts  3.74 us (3%)
    ppermute x29, waiting for transfers between devices, flip(): lax.ppermute(x, axis, [(i, i ^ k) for i in range(lax.axis_size(axis))])  44.4 us
    pallas_call x4, Pallas kernels, gate_up(): pl.pallas_call(functools.partial(gate_up_body, n, chunk, half), out_shape...  32.3 us
    ppermute x29, starting transfers between devices, flip(): lax.ppermute(x, axis, [(i, i ^ k) for i in range(lax.axis_size(axis))])  30.3 us
    pallas_call x4, Pallas kernels, down(): pl.pallas_call(functools.partial(down_body, n_dp, n_out, chunk, first), o...  23.5 us
    unnamed x20, local copies, waits for them, and re-layouts  3.52 us
  transfers between devices with their start and end apart: 29, of which 10 were waited for; matrix products, arithmetic and copies ran while one was open for 3% of the time, Pallas kernels for 31%

profile of v1, /device:TPU:0, one launch (start us, length us, event | category | flops | bytes accessed | tf_op | source)
XLA Modules:
  0.0 141.7 jit_solution(5734232561244109905)
XLA Ops:
  0.0 3.0 %collective-permute-start.3 = (bf16[64,1536]{1,0:T(8,128)(2,1)}, bf16[64,1536]{1,0:T(8,128)(2,1)S(1)}, u32[]{:S(2)}, u32[]{:S(2)}) collective-permute-start(bf16[64,1536]{1,0:T(8,128)(2,1)} %refs_0_.7), channel_id=1, source_target_pairs={{0,4},{4,0},{8,12},{12,8},{1,5},{5,1},{9,13},{13,9},{2,6},{6,2},{1... | collective-permute-start | bytes 589832 | tf_op jit(solution)/shard_map/ppermute | solution.py:21
  3.0 2.6 %collective-permute-start.4 = (bf16[64,1536]{1,0:T(8,128)(2,1)}, bf16[64,1536]{1,0:T(8,128)(2,1)S(1)}, u32[]{:S(2)}, u32[]{:S(2)}) collective-permute-start(bf16[64,1536]{1,0:T(8,128)(2,1)} %refs_0_.7), channel_id=1, source_target_pairs={{0,8},{4,12},{8,0},{12,4},{1,9},{5,13},{9,1},{13,5},{2,10},{6,14},... | collective-permute-start | bytes 589832 | tf_op jit(solution)/shard_map/ppermute | solution.py:21
  7.8 1.0 collective-permute-start
  8.8 3.5 %collective-permute-start.1 = (f32[64,16]{1,0:T(8,128)S(1)}, f32[64,16]{1,0:T(8,128)S(1)}, u32[]{:S(2)}, u32[]{:S(2)}) collective-permute-start(f32[64,16]{1,0:T(8,128)S(1)} %copy.12.refs_0_), channel_id=1, source_target_pairs={{0,8},{4,12},{8,0},{12,4},{1,9},{5,13},{9,1},{13,5},{2,10},{6,14},... | collective-permute-start | bytes 12296 | tf_op jit(solution)/shard_map/ppermute | solution.py:21
  12.3 4.7 %collective-permute-done.refs_1_ = f32[64,16]{1,0:T(8,128)S(1)} collective-permute-done((f32[64,16]{1,0:T(8,128)S(1)}, f32[64,16]{1,0:T(8,128)S(1)}, u32[]{:S(2)}, u32[]{:S(2)}) %collective-permute-start) | collective-permute-done | bytes 4128 | tf_op jit(solution)/shard_map/ppermute | solution.py:21
  16.9 2.5 %collective-permute-start.2 = (f32[64,16]{1,0:T(8,128)S(1)}, f32[64,16]{1,0:T(8,128)S(1)}, u32[]{:S(2)}, u32[]{:S(2)}) collective-permute-start(f32[64,16]{1,0:T(8,128)S(1)} %copy.12.refs_0_), channel_id=1, source_target_pairs={{0,12},{4,8},{8,4},{12,0},{1,13},{5,9},{9,5},{13,1},{2,14},{6,10},... | collective-permute-start | bytes 12296 | tf_op jit(solution)/shard_map/ppermute | solution.py:21
  20.0 5.7 %collective-permute-done.1.refs_2_ = f32[64,16]{1,0:T(8,128)S(1)} collective-permute-done((f32[64,16]{1,0:T(8,128)S(1)}, f32[64,16]{1,0:T(8,128)S(1)}, u32[]{:S(2)}, u32[]{:S(2)}) %collective-permute-start.1) | collective-permute-done | bytes 4128 | tf_op jit(solution)/shard_map/ppermute | solution.py:21
  26.9 2.5 %route.1 = (f32[8,256]{1,0:T(8,128)}, f32[256,128]{1,0:T(8,128)}, f32[256,128]{1,0:T(8,128)}, s32[8,128]{1,0:T(8,128)}) custom-call(s32[2]{0:T(128)} %pad_add_fusion.info, f32[64,16]{1,0:T(8,128)} %copy-done.6, f32[64,16]{1,0:T(8,128)} %copy-done.7, f32[64,16]{1,0:T(8,128)} %copy-done.8, f32[64,16]{1,0:T(8,128)} %copy-done.9), custom_call_target="tpu_custom_call" | custom-call | tf_op jit(solution)/shard_map/route/pallas_call | solution.py:74
  31.7 8.1 %gate_up.7 = (bf16[2,256,512]{2,1,0:T(8,128)(2,1)S(1)}, bf16[2,256,512]{2,1,0:T(8,128)(2,1)S(1)}) custom-call(s32[8,128]{1,0:T(8,128)S(1)} %copy-done.3, bf16[64,1536]{1,0:T(8,128)(2,1)S(1)} %copy-done, bf16[64,1536]{1,0:T(8,128)(2,1)S(1)} %collective-permute-done.3.refs_1_, bf16[64,1536]{1,0:T(8,128)(2,1)S(1)} %collective-permute-done.4.refs_2_, ...), custom_call_target="tpu_custom_call" | custom-call | flops 3221225472 | bytes 12582912 | tf_op jit(solution)/shard_map/gate_up/pallas_call | solution.py:144
  39.8 8.1 %gate_up.6 = (bf16[2,256,512]{2,1,0:T(8,128)(2,1)S(1)}, bf16[2,256,512]{2,1,0:T(8,128)(2,1)S(1)}) custom-call(s32[8,128]{1,0:T(8,128)S(1)} %copy-done.3, bf16[64,1536]{1,0:T(8,128)(2,1)S(1)} %copy-done, bf16[64,1536]{1,0:T(8,128)(2,1)S(1)} %collective-permute-done.3.refs_1_, bf16[64,1536]{1,0:T(8,128)(2,1)S(1)} %collective-permute-done.4.refs_2_, ...), custom_call_target="tpu_custom_call" | custom-call | flops 3221225472 | bytes 12582912 | tf_op jit(solution)/shard_map/gate_up/pallas_call | solution.py:144
  48.5 8.1 %gate_up.5 = (bf16[2,256,512]{2,1,0:T(8,128)(2,1)S(1)}, bf16[2,256,512]{2,1,0:T(8,128)(2,1)S(1)}) custom-call(s32[8,128]{1,0:T(8,128)S(1)} %copy-done.3, bf16[64,1536]{1,0:T(8,128)(2,1)S(1)} %copy-done, bf16[64,1536]{1,0:T(8,128)(2,1)S(1)} %collective-permute-done.3.refs_1_, bf16[64,1536]{1,0:T(8,128)(2,1)S(1)} %collective-permute-done.4.refs_2_, ...), custom_call_target="tpu_custom_call" | custom-call | flops 3221225472 | bytes 12582912 | tf_op jit(solution)/shard_map/gate_up/pallas_call | solution.py:144
  56.7 8.1 %gate_up.4 = (bf16[2,256,512]{2,1,0:T(8,128)(2,1)S(1)}, bf16[2,256,512]{2,1,0:T(8,128)(2,1)S(1)}) custom-call(s32[8,128]{1,0:T(8,128)S(1)} %copy-done.3, bf16[64,1536]{1,0:T(8,128)(2,1)S(1)} %copy-done, bf16[64,1536]{1,0:T(8,128)(2,1)S(1)} %collective-permute-done.3.refs_1_, bf16[64,1536]{1,0:T(8,128)(2,1)S(1)} %collective-permute-done.4.refs_2_, ...), custom_call_target="tpu_custom_call" | custom-call | flops 3221225472 | bytes 12582912 | tf_op jit(solution)/shard_map/gate_up/pallas_call | solution.py:144
  65.5 1.6 %collective-permute-start.22 = (bf16[1,256,512]{2,1,0:T(8,128)(2,1)S(1)}, bf16[1,256,512]{2,1,0:T(8,128)(2,1)S(1)}, u32[]{:S(2)}, u32[]{:S(2)}) collective-permute-start(bf16[1,256,512]{2,1,0:T(8,128)(2,1)S(1)} %slice.116), channel_id=1, source_target_pairs={{0,2},{1,3},{2,0},{3,1},{4,6},{5,7},{6,4},{7,5},{8,10},{9,11},{10,... | collective-permute-start | bytes 786440 | tf_op jit(solution)/shard_map/ppermute | solution.py:21
  68.0 1.6 %collective-permute-start.12 = (bf16[1,256,512]{2,1,0:T(8,128)(2,1)S(1)}, bf16[1,256,512]{2,1,0:T(8,128)(2,1)S(1)}, u32[]{:S(2)}, u32[]{:S(2)}) collective-permute-start(bf16[1,256,512]{2,1,0:T(8,128)(2,1)S(1)} %slice.118), channel_id=1, source_target_pairs={{0,2},{1,3},{2,0},{3,1},{4,6},{5,7},{6,4},{7,5},{8,10},{9,11},{10,... | collective-permute-start | bytes 786440 | tf_op jit(solution)/shard_map/ppermute | solution.py:21
  70.4 4.3 %collective-permute-done.22 = bf16[1,256,512]{2,1,0:T(8,128)(2,1)S(1)} collective-permute-done((bf16[1,256,512]{2,1,0:T(8,128)(2,1)S(1)}, bf16[1,256,512]{2,1,0:T(8,128)(2,1)S(1)}, u32[]{:S(2)}, u32[]{:S(2)}) %collective-permute-start.22) | collective-permute-done | bytes 262176 | tf_op jit(solution)/shard_map/ppermute | solution.py:21
  74.9 1.6 %collective-permute-start.24 = (bf16[1,256,256]{2,1,0:T(8,128)(2,1)S(1)}, bf16[1,256,256]{2,1,0:T(8,128)(2,1)S(1)}, u32[]{:S(2)}, u32[]{:S(2)}) collective-permute-start(bf16[1,256,256]{2,1,0:T(8,128)(2,1)S(1)} %fusion.refs_0_), channel_id=1, source_target_pairs={{0,2},{1,3},{2,0},{3,1},{4,6},{5,7},{6,4},{7,5},{8,10},{9,11},{10,... | collective-permute-start | bytes 393224 | tf_op jit(solution)/shard_map/ppermute | solution.py:21
  76.4 3.9 %collective-permute-done.17 = bf16[1,256,512]{2,1,0:T(8,128)(2,1)S(1)} collective-permute-done((bf16[1,256,512]{2,1,0:T(8,128)(2,1)S(1)}, bf16[1,256,512]{2,1,0:T(8,128)(2,1)S(1)}, u32[]{:S(2)}, u32[]{:S(2)}) %collective-permute-start.17) | collective-permute-done | bytes 262176 | tf_op jit(solution)/shard_map/ppermute | solution.py:21
  80.5 1.6 %collective-permute-start.19 = (bf16[1,256,256]{2,1,0:T(8,128)(2,1)S(1)}, bf16[1,256,256]{2,1,0:T(8,128)(2,1)S(1)}, u32[]{:S(2)}, u32[]{:S(2)}) collective-permute-start(bf16[1,256,256]{2,1,0:T(8,128)(2,1)S(1)} %fusion.1.refs_0_), channel_id=1, source_target_pairs={{0,2},{1,3},{2,0},{3,1},{4,6},{5,7},{6,4},{7,5},{8,10},{9,11},{10,... | collective-permute-start | bytes 393224 | tf_op jit(solution)/shard_map/ppermute | solution.py:21
  82.1 3.9 %collective-permute-done.12 = bf16[1,256,512]{2,1,0:T(8,128)(2,1)S(1)} collective-permute-done((bf16[1,256,512]{2,1,0:T(8,128)(2,1)S(1)}, bf16[1,256,512]{2,1,0:T(8,128)(2,1)S(1)}, u32[]{:S(2)}, u32[]{:S(2)}) %collective-permute-start.12) | collective-permute-done | bytes 262176 | tf_op jit(solution)/shard_map/ppermute | solution.py:21
  86.1 5.4 %collective-permute-done.7 = bf16[1,256,512]{2,1,0:T(8,128)(2,1)S(1)} collective-permute-done((bf16[1,256,512]{2,1,0:T(8,128)(2,1)S(1)}, bf16[1,256,512]{2,1,0:T(8,128)(2,1)S(1)}, u32[]{:S(2)}, u32[]{:S(2)}) %collective-permute-start.7) | collective-permute-done | bytes 262176 | tf_op jit(solution)/shard_map/ppermute | solution.py:21
  91.6 1.5 %collective-permute-start.14 = (bf16[1,256,256]{2,1,0:T(8,128)(2,1)S(1)}, bf16[1,256,256]{2,1,0:T(8,128)(2,1)S(1)}, u32[]{:S(2)}, u32[]{:S(2)}) collective-permute-start(bf16[1,256,256]{2,1,0:T(8,128)(2,1)S(1)} %fusion.2.refs_0_), channel_id=1, source_target_pairs={{0,2},{1,3},{2,0},{3,1},{4,6},{5,7},{6,4},{7,5},{8,10},{9,11},{10,... | collective-permute-start | bytes 393224 | tf_op jit(solution)/shard_map/ppermute | solution.py:21
  93.1 1.2 collective-permute-done.24.refs_2_
  95.0 2.1 %collective-permute-done.19.refs_2_ = bf16[1,256,256]{2,1,0:T(8,128)(2,1)S(1)} collective-permute-done((bf16[1,256,256]{2,1,0:T(8,128)(2,1)S(1)}, bf16[1,256,256]{2,1,0:T(8,128)(2,1)S(1)}, u32[]{:S(2)}, u32[]{:S(2)}) %collective-permute-start.19) | collective-permute-done | bytes 131104 | tf_op jit(solution)/shard_map/ppermute | solution.py:21
  97.2 1.5 %collective-permute-start.9 = (bf16[1,256,256]{2,1,0:T(8,128)(2,1)S(1)}, bf16[1,256,256]{2,1,0:T(8,128)(2,1)S(1)}, u32[]{:S(2)}, u32[]{:S(2)}) collective-permute-start(bf16[1,256,256]{2,1,0:T(8,128)(2,1)S(1)} %fusion.3.refs_0_), channel_id=1, source_target_pairs={{0,2},{1,3},{2,0},{3,1},{4,6},{5,7},{6,4},{7,5},{8,10},{9,11},{10,... | collective-permute-start | bytes 393224 | tf_op jit(solution)/shard_map/ppermute | solution.py:21
  98.7 5.9 %down.4.refs_8_ = f32[256,1536]{1,0:T(8,128)S(1)} custom-call(s32[8,128]{1,0:T(8,128)S(1)} %copy-done.4, bf16[1,256,256]{2,1,0:T(8,128)(2,1)S(1)} %fusion.refs_0_, bf16[1,256,256]{2,1,0:T(8,128)(2,1)S(1)} %collective-permute-done.23.refs_1_, bf16[1,256,256]{2,1,0:T(8,128)(2,1)S(1)} %collective-permute-done.24.refs_2_, ...), custom_call_target="tpu_custom_call" | custom-call | flops 1811939328 | bytes 9437184 | tf_op jit(solution)/shard_map/down/pallas_call | solution.py:220
  105.7 5.9 %down.5.refs_8_ = f32[256,1536]{1,0:T(8,128)S(1)} custom-call(s32[8,128]{1,0:T(8,128)S(1)} %copy-done.4, bf16[1,256,256]{2,1,0:T(8,128)(2,1)S(1)} %fusion.1.refs_0_, bf16[1,256,256]{2,1,0:T(8,128)(2,1)S(1)} %collective-permute-done.18.refs_1_, bf16[1,256,256]{2,1,0:T(8,128)(2,1)S(1)} %collective-permute-done.19.refs_2_, ...), custom_call_target="tpu_custom_call" | custom-call | flops 1811939328 | bytes 9437184 | tf_op jit(solution)/shard_map/down/pallas_call | solution.py:220
  111.6 5.9 %down.6.refs_8_ = f32[256,1536]{1,0:T(8,128)S(1)} custom-call(s32[8,128]{1,0:T(8,128)S(1)} %copy-done.4, bf16[1,256,256]{2,1,0:T(8,128)(2,1)S(1)} %fusion.2.refs_0_, bf16[1,256,256]{2,1,0:T(8,128)(2,1)S(1)} %collective-permute-done.13.refs_1_, bf16[1,256,256]{2,1,0:T(8,128)(2,1)S(1)} %collective-permute-done.14.refs_2_, ...), custom_call_target="tpu_custom_call" | custom-call | flops 1811939328 | bytes 9437184 | tf_op jit(solution)/shard_map/down/pallas_call | solution.py:220
  117.5 5.9 %down.7 = (bf16[64,1536]{1,0:T(8,128)(2,1)S(1)}, bf16[64,1536]{1,0:T(8,128)(2,1)S(1)}, bf16[64,1536]{1,0:T(8,128)(2,1)S(1)}, bf16[64,1536]{1,0:T(8,128)(2,1)S(1)}) custom-call(s32[8,128]{1,0:T(8,128)S(1)} %copy-done.4, bf16[1,256,256]{2,1,0:T(8,128)(2,1)S(1)} %fusion.3.refs_0_, bf16[1,256,256]{2,1,0:T(8,128)(2,1)S(1)} %collective-permute-done.8.refs_1_, ...), custom_call_target="tpu_custom_call" | custom-call | flops 1811939328 | bytes 9437184 | tf_op jit(solution)/shard_map/down/pallas_call | solution.py:220
  123.8 2.7 %collective-permute-start.27 = (bf16[64,1536]{1,0:T(8,128)(2,1)S(1)}, bf16[64,1536]{1,0:T(8,128)(2,1)S(1)}, u32[]{:S(2)}, u32[]{:S(2)}) collective-permute-start(bf16[64,1536]{1,0:T(8,128)(2,1)S(1)} %get-tuple-element.35), channel_id=1, source_target_pairs={{0,8},{4,12},{8,0},{12,4},{1,9},{5,13},{9,1},{13,5},{2,10},{6,14},... | collective-permute-start | bytes 589832 | tf_op jit(solution)/shard_map/ppermute | solution.py:21
  126.5 1.3 collective-permute-start.28
  127.8 6.1 %collective-permute-done.26 = bf16[64,1536]{1,0:T(8,128)(2,1)S(1)} collective-permute-done((bf16[64,1536]{1,0:T(8,128)(2,1)S(1)}, bf16[64,1536]{1,0:T(8,128)(2,1)S(1)}, u32[]{:S(2)}, u32[]{:S(2)}) %collective-permute-start.26) | collective-permute-done | bytes 196640 | tf_op jit(solution)/shard_map/ppermute | solution.py:21
  133.9 7.0 %collective-permute-done.27 = bf16[64,1536]{1,0:T(8,128)(2,1)S(1)} collective-permute-done((bf16[64,1536]{1,0:T(8,128)(2,1)S(1)}, bf16[64,1536]{1,0:T(8,128)(2,1)S(1)}, u32[]{:S(2)}, u32[]{:S(2)}) %collective-permute-start.27) | collective-permute-done | bytes 196640 | tf_op jit(solution)/shard_map/ppermute | solution.py:21
  (78 shorter events, 12.9 us)
Async XLA Ops:
  0.0 29.3 %collective-permute-start.3 = (bf16[64,1536]{1,0:T(8,128)(2,1)}, bf16[64,1536]{1,0:T(8,128)(2,1)S(1)}, u32[]{:S(2)}, u32[]{:S(2)}) collective-permute-start(bf16[64,1536]{1,0:T(8,128)(2,1)} %refs_0_.7), channel_id=1, source_target_pairs={{0,4},{4,0},{8,12},{12,8},{1,5},{5,1},{9,13},{13,9},{2,6},{6,2},{1... | collective-permute-start | bytes 589832 | tf_op jit(solution)/shard_map/ppermute | solution.py:21
  3.0 26.3 %collective-permute-start.4 = (bf16[64,1536]{1,0:T(8,128)(2,1)}, bf16[64,1536]{1,0:T(8,128)(2,1)S(1)}, u32[]{:S(2)}, u32[]{:S(2)}) collective-permute-start(bf16[64,1536]{1,0:T(8,128)(2,1)} %refs_0_.7), channel_id=1, source_target_pairs={{0,8},{4,12},{8,0},{12,4},{1,9},{5,13},{9,1},{13,5},{2,10},{6,14},... | collective-permute-start | bytes 589832 | tf_op jit(solution)/shard_map/ppermute | solution.py:21
  5.6 23.7 %collective-permute-start.5 = (bf16[64,1536]{1,0:T(8,128)(2,1)}, bf16[64,1536]{1,0:T(8,128)(2,1)S(1)}, u32[]{:S(2)}, u32[]{:S(2)}) collective-permute-start(bf16[64,1536]{1,0:T(8,128)(2,1)} %refs_0_.7), channel_id=1, source_target_pairs={{0,12},{4,8},{8,4},{12,0},{1,13},{5,9},{9,5},{13,1},{2,14},{6,10},... | collective-permute-start | bytes 589832 | tf_op jit(solution)/shard_map/ppermute | solution.py:21
  7.8 9.1 %collective-permute-start = (f32[64,16]{1,0:T(8,128)S(1)}, f32[64,16]{1,0:T(8,128)S(1)}, u32[]{:S(2)}, u32[]{:S(2)}) collective-permute-start(f32[64,16]{1,0:T(8,128)S(1)} %copy.12.refs_0_), channel_id=1, source_target_pairs={{0,4},{4,0},{8,12},{12,8},{1,5},{5,1},{9,13},{13,9},{2,6},{6,2},{1... | collective-permute-start | bytes 12296 | tf_op jit(solution)/shard_map/ppermute | solution.py:21
  8.8 16.9 %collective-permute-start.1 = (f32[64,16]{1,0:T(8,128)S(1)}, f32[64,16]{1,0:T(8,128)S(1)}, u32[]{:S(2)}, u32[]{:S(2)}) collective-permute-start(f32[64,16]{1,0:T(8,128)S(1)} %copy.12.refs_0_), channel_id=1, source_target_pairs={{0,8},{4,12},{8,0},{12,4},{1,9},{5,13},{9,1},{13,5},{2,10},{6,14},... | collective-permute-start | bytes 12296 | tf_op jit(solution)/shard_map/ppermute | solution.py:21
  16.9 8.7 %collective-permute-start.2 = (f32[64,16]{1,0:T(8,128)S(1)}, f32[64,16]{1,0:T(8,128)S(1)}, u32[]{:S(2)}, u32[]{:S(2)}) collective-permute-start(f32[64,16]{1,0:T(8,128)S(1)} %copy.12.refs_0_), channel_id=1, source_target_pairs={{0,12},{4,8},{8,4},{12,0},{1,13},{5,9},{9,5},{13,1},{2,14},{6,10},... | collective-permute-start | bytes 12296 | tf_op jit(solution)/shard_map/ppermute | solution.py:21
  39.7 25.5 %collective-permute-start.21 = (bf16[2,256,512]{2,1,0:T(8,128)(2,1)S(1)}, bf16[2,256,512]{2,1,0:T(8,128)(2,1)S(1)}, u32[]{:S(2)}, u32[]{:S(2)}) collective-permute-start(bf16[2,256,512]{2,1,0:T(8,128)(2,1)S(1)} %get-tuple-element.32), channel_id=1, source_target_pairs={{0,1},{1,0},{2,3},{3,2},{4,5},{5,4},{6,7},{7,6},{8,9},{9,8},{10,11... | collective-permute-start | bytes 1572872 | tf_op jit(solution)/shard_map/ppermute | solution.py:21
  47.9 19.1 %collective-permute-start.16 = (bf16[2,256,512]{2,1,0:T(8,128)(2,1)S(1)}, bf16[2,256,512]{2,1,0:T(8,128)(2,1)S(1)}, u32[]{:S(2)}, u32[]{:S(2)}) collective-permute-start(bf16[2,256,512]{2,1,0:T(8,128)(2,1)S(1)} %get-tuple-element.30), channel_id=1, source_target_pairs={{0,1},{1,0},{2,3},{3,2},{4,5},{5,4},{6,7},{7,6},{8,9},{9,8},{10,11... | collective-permute-start | bytes 1572872 | tf_op jit(solution)/shard_map/ppermute | solution.py:21
  56.5 42.2 %copy-start.1 = (f32[256,128]{1,0:T(8,128)S(1)}, f32[256,128]{1,0:T(8,128)}, u32[]{:S(2)}) copy-start(f32[256,128]{1,0:T(8,128)} %get-tuple-element.25.refs_4_) | copy-start | bytes 393220
  56.5 42.1 %copy-start.2 = (f32[256,128]{1,0:T(8,128)S(1)}, f32[256,128]{1,0:T(8,128)}, u32[]{:S(2)}) copy-start(f32[256,128]{1,0:T(8,128)} %get-tuple-element.26.refs_5_) | copy-start | bytes 393220
  56.6 42.1 %copy-start.4 = (s32[8,128]{1,0:T(8,128)S(1)}, s32[8,128]{1,0:T(8,128)}, u32[]{:S(2)}) copy-start(s32[8,128]{1,0:T(8,128)} %get-tuple-element.21.sched) | copy-start | bytes 12292
  56.6 11.3 %collective-permute-start.11 = (bf16[2,256,512]{2,1,0:T(8,128)(2,1)S(1)}, bf16[2,256,512]{2,1,0:T(8,128)(2,1)S(1)}, u32[]{:S(2)}, u32[]{:S(2)}) collective-permute-start(bf16[2,256,512]{2,1,0:T(8,128)(2,1)S(1)} %get-tuple-element.28), channel_id=1, source_target_pairs={{0,1},{1,0},{2,3},{3,2},{4,5},{5,4},{6,7},{7,6},{8,9},{9,8},{10,11... | collective-permute-start | bytes 1572872 | tf_op jit(solution)/shard_map/ppermute | solution.py:21
  64.7 4.9 %collective-permute-start.6 = (bf16[2,256,512]{2,1,0:T(8,128)(2,1)S(1)}, bf16[2,256,512]{2,1,0:T(8,128)(2,1)S(1)}, u32[]{:S(2)}, u32[]{:S(2)}) collective-permute-start(bf16[2,256,512]{2,1,0:T(8,128)(2,1)S(1)} %get-tuple-element.24), channel_id=1, source_target_pairs={{0,1},{1,0},{2,3},{3,2},{4,5},{5,4},{6,7},{7,6},{8,9},{9,8},{10,11... | collective-permute-start | bytes 1572872 | tf_op jit(solution)/shard_map/ppermute | solution.py:21
  65.5 9.2 %collective-permute-start.22 = (bf16[1,256,512]{2,1,0:T(8,128)(2,1)S(1)}, bf16[1,256,512]{2,1,0:T(8,128)(2,1)S(1)}, u32[]{:S(2)}, u32[]{:S(2)}) collective-permute-start(bf16[1,256,512]{2,1,0:T(8,128)(2,1)S(1)} %slice.116), channel_id=1, source_target_pairs={{0,2},{1,3},{2,0},{3,1},{4,6},{5,7},{6,4},{7,5},{8,10},{9,11},{10,... | collective-permute-start | bytes 786440 | tf_op jit(solution)/shard_map/ppermute | solution.py:21
  67.2 13.1 %collective-permute-start.17 = (bf16[1,256,512]{2,1,0:T(8,128)(2,1)S(1)}, bf16[1,256,512]{2,1,0:T(8,128)(2,1)S(1)}, u32[]{:S(2)}, u32[]{:S(2)}) collective-permute-start(bf16[1,256,512]{2,1,0:T(8,128)(2,1)S(1)} %slice.117), channel_id=1, source_target_pairs={{0,2},{1,3},{2,0},{3,1},{4,6},{5,7},{6,4},{7,5},{8,10},{9,11},{10,... | collective-permute-start | bytes 786440 | tf_op jit(solution)/shard_map/ppermute | solution.py:21
  68.0 17.9 %collective-permute-start.12 = (bf16[1,256,512]{2,1,0:T(8,128)(2,1)S(1)}, bf16[1,256,512]{2,1,0:T(8,128)(2,1)S(1)}, u32[]{:S(2)}, u32[]{:S(2)}) collective-permute-start(bf16[1,256,512]{2,1,0:T(8,128)(2,1)S(1)} %slice.118), channel_id=1, source_target_pairs={{0,2},{1,3},{2,0},{3,1},{4,6},{5,7},{6,4},{7,5},{8,10},{9,11},{10,... | collective-permute-start | bytes 786440 | tf_op jit(solution)/shard_map/ppermute | solution.py:21
  69.8 21.8 %collective-permute-start.7 = (bf16[1,256,512]{2,1,0:T(8,128)(2,1)S(1)}, bf16[1,256,512]{2,1,0:T(8,128)(2,1)S(1)}, u32[]{:S(2)}, u32[]{:S(2)}) collective-permute-start(bf16[1,256,512]{2,1,0:T(8,128)(2,1)S(1)} %slice.119), channel_id=1, source_target_pairs={{0,2},{1,3},{2,0},{3,1},{4,6},{5,7},{6,4},{7,5},{8,10},{9,11},{10,... | collective-permute-start | bytes 786440 | tf_op jit(solution)/shard_map/ppermute | solution.py:21
  74.9 19.5 %collective-permute-start.24 = (bf16[1,256,256]{2,1,0:T(8,128)(2,1)S(1)}, bf16[1,256,256]{2,1,0:T(8,128)(2,1)S(1)}, u32[]{:S(2)}, u32[]{:S(2)}) collective-permute-start(bf16[1,256,256]{2,1,0:T(8,128)(2,1)S(1)} %fusion.refs_0_), channel_id=1, source_target_pairs={{0,2},{1,3},{2,0},{3,1},{4,6},{5,7},{6,4},{7,5},{8,10},{9,11},{10,... | collective-permute-start | bytes 393224 | tf_op jit(solution)/shard_map/ppermute | solution.py:21
  76.4 18.0 %collective-permute-start.23 = (bf16[1,256,256]{2,1,0:T(8,128)(2,1)S(1)}, bf16[1,256,256]{2,1,0:T(8,128)(2,1)S(1)}, u32[]{:S(2)}, u32[]{:S(2)}) collective-permute-start(bf16[1,256,256]{2,1,0:T(8,128)(2,1)S(1)} %fusion.refs_0_), channel_id=1, source_target_pairs={{0,1},{1,0},{2,3},{3,2},{4,5},{5,4},{6,7},{7,6},{8,9},{9,8},{10,11... | collective-permute-start | bytes 393224 | tf_op jit(solution)/shard_map/ppermute | solution.py:21
  80.5 16.7 %collective-permute-start.19 = (bf16[1,256,256]{2,1,0:T(8,128)(2,1)S(1)}, bf16[1,256,256]{2,1,0:T(8,128)(2,1)S(1)}, u32[]{:S(2)}, u32[]{:S(2)}) collective-permute-start(bf16[1,256,256]{2,1,0:T(8,128)(2,1)S(1)} %fusion.1.refs_0_), channel_id=1, source_target_pairs={{0,2},{1,3},{2,0},{3,1},{4,6},{5,7},{6,4},{7,5},{8,10},{9,11},{10,... | collective-permute-start | bytes 393224 | tf_op jit(solution)/shard_map/ppermute | solution.py:21
  85.9 18.7 %collective-permute-start.18 = (bf16[1,256,256]{2,1,0:T(8,128)(2,1)S(1)}, bf16[1,256,256]{2,1,0:T(8,128)(2,1)S(1)}, u32[]{:S(2)}, u32[]{:S(2)}) collective-permute-start(bf16[1,256,256]{2,1,0:T(8,128)(2,1)S(1)} %fusion.1.refs_0_), channel_id=1, source_target_pairs={{0,1},{1,0},{2,3},{3,2},{4,5},{5,4},{6,7},{7,6},{8,9},{9,8},{10,11... | collective-permute-start | bytes 393224 | tf_op jit(solution)/shard_map/ppermute | solution.py:21
  91.6 13.6 %collective-permute-start.14 = (bf16[1,256,256]{2,1,0:T(8,128)(2,1)S(1)}, bf16[1,256,256]{2,1,0:T(8,128)(2,1)S(1)}, u32[]{:S(2)}, u32[]{:S(2)}) collective-permute-start(bf16[1,256,256]{2,1,0:T(8,128)(2,1)S(1)} %fusion.2.refs_0_), channel_id=1, source_target_pairs={{0,2},{1,3},{2,0},{3,1},{4,6},{5,7},{6,4},{7,5},{8,10},{9,11},{10,... | collective-permute-start | bytes 393224 | tf_op jit(solution)/shard_map/ppermute | solution.py:21
  94.4 4.3 %collective-permute-start.25 = (bf16[1,256,256]{2,1,0:T(8,128)(2,1)S(1)}, bf16[1,256,256]{2,1,0:T(8,128)(2,1)S(1)}, u32[]{:S(2)}, u32[]{:S(2)}) collective-permute-start(bf16[1,256,256]{2,1,0:T(8,128)(2,1)S(1)} %collective-permute-done.24.refs_2_), channel_id=1, source_target_pairs={{0,1},{1,0},{2,3},{3,2},{4,5},{5,4},{6,7},{7,6},{8,9},{9,8},{10,11... | collective-permute-start | bytes 393224 | tf_op jit(solution)/shard_map/ppermute | solution.py:21
  94.5 17.1 %collective-permute-start.13 = (bf16[1,256,256]{2,1,0:T(8,128)(2,1)S(1)}, bf16[1,256,256]{2,1,0:T(8,128)(2,1)S(1)}, u32[]{:S(2)}, u32[]{:S(2)}) collective-permute-start(bf16[1,256,256]{2,1,0:T(8,128)(2,1)S(1)} %fusion.2.refs_0_), channel_id=1, source_target_pairs={{0,1},{1,0},{2,3},{3,2},{4,5},{5,4},{6,7},{7,6},{8,9},{9,8},{10,11... | collective-permute-start | bytes 393224 | tf_op jit(solution)/shard_map/ppermute | solution.py:21
  97.2 8.1 %collective-permute-start.9 = (bf16[1,256,256]{2,1,0:T(8,128)(2,1)S(1)}, bf16[1,256,256]{2,1,0:T(8,128)(2,1)S(1)}, u32[]{:S(2)}, u32[]{:S(2)}) collective-permute-start(bf16[1,256,256]{2,1,0:T(8,128)(2,1)S(1)} %fusion.3.refs_0_), channel_id=1, source_target_pairs={{0,2},{1,3},{2,0},{3,1},{4,6},{5,7},{6,4},{7,5},{8,10},{9,11},{10,... | collective-permute-start | bytes 393224 | tf_op jit(solution)/shard_map/ppermute | solution.py:21
  98.7 7.0 %collective-permute-start.20 = (bf16[1,256,256]{2,1,0:T(8,128)(2,1)S(1)}, bf16[1,256,256]{2,1,0:T(8,128)(2,1)S(1)}, u32[]{:S(2)}, u32[]{:S(2)}) collective-permute-start(bf16[1,256,256]{2,1,0:T(8,128)(2,1)S(1)} %collective-permute-done.19.refs_2_), channel_id=1, source_target_pairs={{0,1},{1,0},{2,3},{3,2},{4,5},{5,4},{6,7},{7,6},{8,9},{9,8},{10,11... | collective-permute-start | bytes 393224 | tf_op jit(solution)/shard_map/ppermute | solution.py:21
  104.6 12.9 %collective-permute-start.8 = (bf16[1,256,256]{2,1,0:T(8,128)(2,1)S(1)}, bf16[1,256,256]{2,1,0:T(8,128)(2,1)S(1)}, u32[]{:S(2)}, u32[]{:S(2)}) collective-permute-start(bf16[1,256,256]{2,1,0:T(8,128)(2,1)S(1)} %fusion.3.refs_0_), channel_id=1, source_target_pairs={{0,1},{1,0},{2,3},{3,2},{4,5},{5,4},{6,7},{7,6},{8,9},{9,8},{10,11... | collective-permute-start | bytes 393224 | tf_op jit(solution)/shard_map/ppermute | solution.py:21
  105.2 6.4 %collective-permute-start.15 = (bf16[1,256,256]{2,1,0:T(8,128)(2,1)S(1)}, bf16[1,256,256]{2,1,0:T(8,128)(2,1)S(1)}, u32[]{:S(2)}, u32[]{:S(2)}) collective-permute-start(bf16[1,256,256]{2,1,0:T(8,128)(2,1)S(1)} %collective-permute-done.14.refs_2_), channel_id=1, source_target_pairs={{0,1},{1,0},{2,3},{3,2},{4,5},{5,4},{6,7},{7,6},{8,9},{9,8},{10,11... | collective-permute-start | bytes 393224 | tf_op jit(solution)/shard_map/ppermute | solution.py:21
  105.3 12.2 %collective-permute-start.10 = (bf16[1,256,256]{2,1,0:T(8,128)(2,1)S(1)}, bf16[1,256,256]{2,1,0:T(8,128)(2,1)S(1)}, u32[]{:S(2)}, u32[]{:S(2)}) collective-permute-start(bf16[1,256,256]{2,1,0:T(8,128)(2,1)S(1)} %collective-permute-done.9.refs_2_), channel_id=1, source_target_pairs={{0,1},{1,0},{2,3},{3,2},{4,5},{5,4},{6,7},{7,6},{8,9},{9,8},{10,11... | collective-permute-start | bytes 393224 | tf_op jit(solution)/shard_map/ppermute | solution.py:21
  123.4 10.5 %collective-permute-start.26 = (bf16[64,1536]{1,0:T(8,128)(2,1)S(1)}, bf16[64,1536]{1,0:T(8,128)(2,1)S(1)}, u32[]{:S(2)}, u32[]{:S(2)}) collective-permute-start(bf16[64,1536]{1,0:T(8,128)(2,1)S(1)} %get-tuple-element.34), channel_id=1, source_target_pairs={{0,4},{4,0},{8,12},{12,8},{1,5},{5,1},{9,13},{13,9},{2,6},{6,2},{1... | collective-permute-start | bytes 589832 | tf_op jit(solution)/shard_map/ppermute | solution.py:21
  123.8 17.1 %collective-permute-start.27 = (bf16[64,1536]{1,0:T(8,128)(2,1)S(1)}, bf16[64,1536]{1,0:T(8,128)(2,1)S(1)}, u32[]{:S(2)}, u32[]{:S(2)}) collective-permute-start(bf16[64,1536]{1,0:T(8,128)(2,1)S(1)} %get-tuple-element.35), channel_id=1, source_target_pairs={{0,8},{4,12},{8,0},{12,4},{1,9},{5,13},{9,1},{13,5},{2,10},{6,14},... | collective-permute-start | bytes 589832 | tf_op jit(solution)/shard_map/ppermute | solution.py:21
  126.5 14.4 %collective-permute-start.28 = (bf16[64,1536]{1,0:T(8,128)(2,1)S(1)}, bf16[64,1536]{1,0:T(8,128)(2,1)S(1)}, u32[]{:S(2)}, u32[]{:S(2)}) collective-permute-start(bf16[64,1536]{1,0:T(8,128)(2,1)S(1)} %get-tuple-element.36), channel_id=1, source_target_pairs={{0,12},{4,8},{8,4},{12,0},{1,13},{5,9},{9,5},{13,1},{2,14},{6,10},... | collective-permute-start | bytes 589832 | tf_op jit(solution)/shard_map/ppermute | solution.py:21
  (7 other events, 30.1 us)
